TPU v7x, 128 devices: a whole 4x4x4 slice. The times are simulated.
128 devices in a mesh: wide: 32 (over y, x, z_hi), blk: 4 (over z_lo, core).
Axes of the slice: x: 4, y: 4, z: 4 (z_hi: 2, z_lo: 2; z = z_hi * 2 + z_lo), core: 2. Of those that a mesh axis runs over, the one named last changes fastest.
Arguments:
- visual_features: bfloat16 [131072, 1152], P(('wide', 'blk')), may hold values from -0.1875 to 0.1875
- sentence_features: bfloat16 [4096, 1152], P(('wide', 'blk')), may hold values from -0.1875 to 0.1875
- true_partner_ids: int32 [131072], P(('wide', 'blk')), may hold values from 0 to 4095
- inverse_warmth: float32 [], replicated, may hold values from 90 to 110
- additive_adjust: float32 [], replicated, may hold values from -12 to -9
Outputs:
- grad_images: float32 [131072, 1152], P(('wide', 'blk'))
- grad_texts: float32 [4096, 1152], P(('wide', 'blk'))
Inputs may be any that keep to these rules, and one draw needn't show every extreme that they name: Image i is paired with text true_partner_ids[i]; a text may be paired with several images or none.
All inputs are finite; a program needn't handle non-finite values.
Results may differ from a plain program's by a relative error of at most 0.007.
Values may be sent and summed in bfloat16 or wider, within the bound.
A program may use at most 64 MiB of HBM per device.

v0:
```python
import jax
import jax.numpy as jnp
from jax import lax
from jax.sharding import PartitionSpec as P

AXES = ("wide", "blk")


def shards(images, texts, partners, scale, bias):
    joined = lax.all_gather(texts, AXES, axis=0, tiled=True)
    scores = lax.dot_general(
        images, joined, (((1,), (1,)), ((), ())), preferred_element_type=jnp.float32
    )
    logits = scale * scores + bias
    columns = lax.iota(jnp.int32, joined.shape[0])
    sign = jnp.where(partners[:, None] == columns[None, :], 1.0, -1.0).astype(jnp.float32)
    weights = (-scale * sign * jax.nn.sigmoid(-sign * logits)).astype(jnp.bfloat16)
    grad_images = jnp.dot(weights, joined, preferred_element_type=jnp.float32)
    part = lax.dot_general(
        weights, images, (((0,), (0,)), ((), ())), preferred_element_type=jnp.float32
    )
    grad_texts = lax.psum_scatter(
        part.astype(jnp.bfloat16), AXES, scatter_dimension=0, tiled=True
    ).astype(jnp.float32)
    return (grad_images, grad_texts)


def solution(mesh):
    return jax.shard_map(
        shards,
        mesh=mesh,
        in_specs=(P(AXES, None), P(AXES, None), P(AXES), P(), P()),
        out_specs=(P(AXES, None), P(AXES, None)),
        check_vma=False,
    )
```

profile of v0, /device:TPU:0, one launch (start us, length us, event | category | flops | bytes accessed | tf_op | source)
XLA Modules:
  0.0 343.1 jit_solution(3602282821613848416)
XLA Ops:
  7.2 0.0 copy-start
  7.2 0.0 all-gather.2.cloned.1.call-start
  7.2 0.7 all-gather.2.cloned.1.call-update
  7.9 0.0 reduce-scatter.2.cloned.1.call-start
  9.3 75.2 %all-gather.2.cloned.1.call-done = bf16[4096,1152]{1,0:T(8,128)(2,1)} async-done(((bf16[32,1152]{1,0:T(8,128)(2,1)}), bf16[4096,1152]{1,0:T(8,128)(2,1)}) %all-gather.2.cloned.1.call-update) | async-done | bytes 9437200 | tf_op jit(solution)/shard_map/all_gather | solution.py:10
  84.4 0.0 copy-done
  84.4 19.9 %fusion.1 = bf16[1024,4096]{1,0:T(8,128)(2,1)} fusion(bf16[1024,1152]{1,0:T(8,128)(2,1)S(1)} %copy-done, bf16[4096,1152]{1,0:T(8,128)(2,1)} %all-gather.2.cloned.1.call-done, f32[]{:T(128)S(6)} %copy.8, f32[]{:T(128)S(6)} %copy.7, s32[1024]{0:T(1024)} %param.7, f32[]{:T(128)S(6)} %neg.9), kind=kOutput, calls=%fused_computation.3 | convolution fusion | flops 9714008064 | bytes 20189196 | tf_op jit(solution)/shard_map/dot_general | solution.py:11
  104.4 15.7 %convolution_convert_fusion = bf16[4096,1152]{1,0:T(8,128)(2,1)} fusion(bf16[1024,4096]{1,0:T(8,128)(2,1)} %fusion.1, bf16[1024,1152]{1,0:T(8,128)(2,1)S(1)} %copy-done), kind=kOutput, calls=%fused_computation.10 | convolution fusion | flops 9668395008 | bytes 20185088 | tf_op jit(solution)/shard_map/dot_general | solution.py:19
  120.0 0.0 reduce-scatter.2.cloned.1.call-update
  120.1 17.7 %fusion.7 = f32[1024,1152]{1,0:T(8,128)} fusion(bf16[1024,4096]{1,0:T(8,128)(2,1)} %fusion.1, bf16[4096,1152]{1,0:T(8,128)(2,1)} %all-gather.2.cloned.1.call-done), kind=kOutput, calls=%fused_computation.11 | convolution fusion | flops 9663676416 | bytes 22544384 | tf_op jit(solution)/shard_map/dot_general | solution.py:18
  137.8 197.0 %reduce-scatter.2.cloned.1.call-done = bf16[32,1152]{1,0:T(8,128)(2,1)} async-done(((bf16[4096,1152]{1,0:T(8,128)(2,1)}), bf16[32,1152]{1,0:T(8,128)(2,1)}) %reduce-scatter.2.cloned.1.call-update) | async-done | bytes 73744 | tf_op jit(solution)/shard_map/reduce_scatter | solution.py:22
  334.7 1.6 convert_element_type.11
Async XLA Ops:
  7.2 77.3 %copy-start = (bf16[1024,1152]{1,0:T(8,128)(2,1)S(1)}, bf16[1024,1152]{1,0:T(8,128)(2,1)}, u32[]{:S(2)}) copy-start(bf16[1024,1152]{1,0:T(8,128)(2,1)} %param.5) | copy-start | bytes 7077892
  7.2 77.2 %all-gather.2.cloned.1.call-start = ((), (), s32[]{:S(2)}) async-start(), calls=%async_computation.1 | async-start | bytes 9510912 | tf_op jit(solution)/shard_map/all_gather | solution.py:10
  7.9 326.8 %reduce-scatter.2.cloned.1.call-start = ((), (), s32[]{:S(2)}) async-start(), calls=%async_computation.2 | async-start | bytes 9510912 | tf_op jit(solution)/shard_map/reduce_scatter | solution.py:22
Sparse Core Ops, SparseCore 0:
  11.0 73.3 all-gather.1
  120.2 214.4 reduce-scatter.1
where the time goes:
time: 343 us
  waiting for transfers between devices  273 us (80%)
  matrix products  53.3 us (16%)
  between operations  15.3 us (4%)
    reduce_scatter x1, waiting for transfers between devices, shards(): lax.psum_scatter(part.astype(jnp.bfloat16), AXES, scatter_dimension=0, ti...  197 us
    all_gather x1, waiting for transfers between devices, shards(): joined = lax.all_gather(texts, AXES, axis=0, tiled=True)  75.2 us
    dot_general x1, matrix products, shards(): lax.dot_general(images, joined, (((1,), (1,)), ((), ())), preferred_eleme...  19.9 us
    dot_general x1, matrix products, shards(): grad_images = jnp.dot(weights, joined, preferred_element_type=jnp.float32)  17.7 us
    dot_general x1, matrix products, shards(): lax.dot_general(weights, images, (((0,), (0,)), ((), ())), preferred_elem...  15.7 us
  transfers between devices with their start and end apart: 2, of which 2 were waited for; matrix products, arithmetic and copies ran while one was open for 5% of the time, Pallas kernels for 0%

commit v1 on v0

--- a/solution.py
+++ b/solution.py
@@ -7,7 +7,12 @@
 
 
 def shards(images, texts, partners, scale, bias):
-    joined = lax.all_gather(texts, AXES, axis=0, tiled=True)
+    joined = jnp.concatenate(
+        lax.all_to_all(
+            jnp.stack(lax.axis_size(AXES) * [texts]), axis_name=AXES, split_axis=0, concat_axis=0
+        ),
+        axis=0,
+    )
     scores = lax.dot_general(
         images, joined, (((1,), (1,)), ((), ())), preferred_element_type=jnp.float32
     )

time: 343 us -> 403 us (1.17)
  waiting for transfers between devices: 273 us -> 315 us
  starting transfers between devices: 0.08 us -> 11.7 us
  local copies, waits for them, and re-layouts: 0.01 us -> 5.35 us
    all_to_all x0 -> x1, waiting for transfers between devices: none -> 113 us  [shards(): lax.all_to_all(jnp.stack(lax.axis_size(AXES) * [texts]), axis_name=AXES,...]
    all_gather x1 -> x0, waiting for transfers between devices: 75.2 us -> none  [shards(): joined = lax.all_gather(texts, AXES, axis=0, tiled=True)]
    all_to_all x0 -> x1, starting transfers between devices: none -> 11.6 us  [shards(): lax.all_to_all(jnp.stack(lax.axis_size(AXES) * [texts]), axis_name=AXES,...]
    another operation x0 -> x1, local copies, waits for them, and re-layouts: none -> 5.34 us  [shards(): jnp.stack(lax.axis_size(AXES) * [texts])]
    reduce_scatter x1, waiting for transfers between devices: 197 us -> 202 us  [shards(): lax.psum_scatter(part.astype(jnp.bfloat16), AXES, scatter_dimension=0, ti...]
  transfers between devices with their start and end apart: 2 -> 2, of which waited for: 2 -> 2; matrix products, arithmetic and copies ran while one was open for 5% -> 4% of each run, Pallas kernels for 0% -> 0%
where the time goes in v1:
time: 403 us; the launch traced here: 402 us
  waiting for transfers between devices  315 us (78%)
  matrix products  53.3 us (13%)
  between operations  15.3 us (4%)
  starting transfers between devices  11.7 us (3%)
  local copies, waits for them, and re-layouts  5.35 us (1%)
    reduce_scatter x1, waiting for transfers between devices, shards(): lax.psum_scatter(part.astype(jnp.bfloat16), AXES, scatter_dimension=0, ti...  202 us
    all_to_all x1, waiting for transfers between devices, shards(): lax.all_to_all(jnp.stack(lax.axis_size(AXES) * [texts]), axis_name=AXES,...  113 us
    dot_general x1, matrix products, shards(): lax.dot_general(images, joined, (((1,), (1,)), ((), ())), preferred_eleme...  19.9 us
    dot_general x1, matrix products, shards(): grad_images = jnp.dot(weights, joined, preferred_element_type=jnp.float32)  17.7 us
    dot_general x1, matrix products, shards(): lax.dot_general(weights, images, (((0,), (0,)), ((), ())), preferred_elem...  15.7 us
    all_to_all x1, starting transfers between devices, shards(): lax.all_to_all(jnp.stack(lax.axis_size(AXES) * [texts]), axis_name=AXES,...  11.6 us
  transfers between devices with their start and end apart: 2, of which 2 were waited for; matrix products, arithmetic and copies ran while one was open for 4% of the time, Pallas kernels for 0%

profile of v1, /device:TPU:0, one launch (start us, length us, event | category | flops | bytes accessed | tf_op | source)
XLA Modules:
  0.0 402.3 jit_solution(3173724109755298490)
XLA Ops:
  7.2 0.0 copy-start
  7.2 5.3 %stack.2 = bf16[128,32,1152]{2,1,0:T(8,128)(2,1)} broadcast(bf16[32,1152]{1,0:T(8,128)(2,1)} %param.6), dimensions={1,2} | broadcast | bytes 9510912 | tf_op jit(solution)/shard_map/stack | solution.py:12
  12.5 0.0 copy-start.1
  12.5 11.6 %all-to-all-start = ((bf16[128,32,1152]{2,1,0:T(8,128)(2,1)}), bf16[128,32,1152]{2,1,0:T(8,128)(2,1)}, u32[]{:S(2)}, u32[]{:S(2)}) async-start(bf16[128,32,1152]{2,1,0:T(8,128)(2,1)} %stack.2), calls=%async_computation | async-start | bytes 18874368 | tf_op jit(solution)/shard_map/all_to_all | solution.py:11
  24.1 0.0 reduce-scatter.2.cloned.1.call-start
  25.5 113.4 %all-to-all-done = bf16[128,32,1152]{2,1,0:T(8,128)(2,1)} async-done(((bf16[128,32,1152]{2,1,0:T(8,128)(2,1)}), bf16[128,32,1152]{2,1,0:T(8,128)(2,1)}, u32[]{:S(2)}, u32[]{:S(2)}) %all-to-all-start) | async-done | bytes 9437216 | tf_op jit(solution)/shard_map/all_to_all | solution.py:11
  138.9 0.0 copy-done
  138.9 0.0 copy-done.1
  138.9 19.9 %fusion.1 = bf16[1024,4096]{1,0:T(8,128)(2,1)} fusion(bf16[1024,1152]{1,0:T(8,128)(2,1)S(1)} %copy-done, bf16[4096,1152]{1,0:T(8,128)(2,1)} %bitcast, f32[]{:T(128)S(6)} %copy.8, f32[]{:T(128)S(6)} %copy.7, s32[1024]{0:T(1024)S(1)} %copy-done.1, f32[]{:T(128)S(6)} %neg.9), kind=kOutput, calls=%fused_computation.3 | convolution fusion | flops 9714008064 | bytes 20189196 | tf_op jit(solution)/shard_map/dot_general | solution.py:16
  158.8 15.7 %convolution_convert_fusion = bf16[4096,1152]{1,0:T(8,128)(2,1)} fusion(bf16[1024,4096]{1,0:T(8,128)(2,1)} %fusion.1, bf16[1024,1152]{1,0:T(8,128)(2,1)S(1)} %copy-done), kind=kOutput, calls=%fused_computation.10 | convolution fusion | flops 9668395008 | bytes 20185088 | tf_op jit(solution)/shard_map/dot_general | solution.py:24
  174.5 0.0 reduce-scatter.2.cloned.1.call-update
  174.5 17.7 %fusion.7 = f32[1024,1152]{1,0:T(8,128)} fusion(bf16[1024,4096]{1,0:T(8,128)(2,1)} %fusion.1, bf16[4096,1152]{1,0:T(8,128)(2,1)} %bitcast), kind=kOutput, calls=%fused_computation.11 | convolution fusion | flops 9663676416 | bytes 22544384 | tf_op jit(solution)/shard_map/dot_general | solution.py:23
  192.2 201.6 %reduce-scatter.2.cloned.1.call-done = bf16[32,1152]{1,0:T(8,128)(2,1)} async-done(((bf16[4096,1152]{1,0:T(8,128)(2,1)}), bf16[32,1152]{1,0:T(8,128)(2,1)}) %reduce-scatter.2.cloned.1.call-update) | async-done | bytes 73744 | tf_op jit(solution)/shard_map/reduce_scatter | solution.py:27
  393.9 1.6 convert_element_type.11
Async XLA Ops:
  7.2 131.8 %copy-start = (bf16[1024,1152]{1,0:T(8,128)(2,1)S(1)}, bf16[1024,1152]{1,0:T(8,128)(2,1)}, u32[]{:S(2)}) copy-start(bf16[1024,1152]{1,0:T(8,128)(2,1)} %param.5) | copy-start | bytes 7077892
  12.5 126.4 %copy-start.1 = (s32[1024]{0:T(1024)S(1)}, s32[1024]{0:T(1024)}, u32[]{:S(2)}) copy-start(s32[1024]{0:T(1024)} %param.7) | copy-start | bytes 12292
  12.5 126.4 %all-to-all-start = ((bf16[128,32,1152]{2,1,0:T(8,128)(2,1)}), bf16[128,32,1152]{2,1,0:T(8,128)(2,1)}, u32[]{:S(2)}, u32[]{:S(2)}) async-start(bf16[128,32,1152]{2,1,0:T(8,128)(2,1)} %stack.2), calls=%async_computation | async-start | bytes 18874368 | tf_op jit(solution)/shard_map/all_to_all | solution.py:11
  24.1 369.7 %reduce-scatter.2.cloned.1.call-start = ((), (), s32[]{:S(2)}) async-start(), calls=%async_computation.2 | async-start | bytes 9510912 | tf_op jit(solution)/shard_map/reduce_scatter | solution.py:27
Sparse Core Ops, SparseCore 0:
  174.6 219.1 reduce-scatter.1
